TPU v7x, 32 devices: a whole 2x2x4 slice. The times are simulated.
32 devices in a mesh: blk: 8 (over y, x, core), rows: 4 (over z).
Axes of the slice: x: 2, y: 2, z: 4, core: 2. Of those that a mesh axis runs over, the one named last changes fastest.
Arguments:
- excitations: float32 [64, 16384], P(None, ('blk', 'rows')), may hold values from -6 to 6
- adjoint_loads: float32 [64, 16384], P(None, ('blk', 'rows')), may hold values from -6 to 6
- near_tiles: bfloat16 [1024, 256, 256], P(('blk', 'rows')), may hold values from -0.125 to 0.125
- tile_rows: int32 [1024], P(('blk', 'rows')), may hold values from 0 to 1
- tile_cols: int32 [1024], P(('blk', 'rows')), may hold values from 0 to 7
- tile_count: int32 [32], P(('blk', 'rows')), may hold values from 4 to 32, as said below
- skeleton_in: bfloat16 [1024, 16384], P(None, ('blk', 'rows')), may hold values from -0.125 to 0.125
- skeleton_out: bfloat16 [1024, 16384], P(None, ('blk', 'rows')), may hold values from -0.1875 to 0.1875
- translation: float32 [8, 7, 1024, 1024], P('blk', None, 'rows'), may hold values from -0.0625 to 0.0625
Outputs:
- response: float32 [64, 16384], P(None, ('blk', 'rows'))
- sensitivity: float32 [64, 16384], P(None, ('blk', 'rows'))
Inputs may be any that keep to these rules, and one draw needn't show every extreme that they name: `tile_count`: slots of a device are used from slot 0 on; later slots are no part of the operator.
All inputs are finite; a program needn't handle non-finite values.
Results may differ from a plain program's by a relative error of at most 0.0036.
Values may be sent and summed in bfloat16 or wider, within the bound.
A program may use at most 128 MiB of HBM per device.

v0:
```python
import jax
import jax.numpy as jnp
from jax import lax
from jax.sharding import PartitionSpec as P

highest = lax.Precision.HIGHEST


def on_device(
    excitations,
    adjoint_loads,
    near_tiles,
    tile_rows,
    tile_cols,
    tile_count,
    skeleton_in,
    skeleton_out,
    translation,
):
    drive_low = excitations.astype(jnp.bfloat16)
    loads_low = adjoint_loads.astype(jnp.bfloat16)
    excite_count = excitations.shape[0]
    panels = excitations.shape[1]
    tile_size = near_tiles.shape[1]
    kernels = translation[0]
    share_width = kernels.shape[1]
    clusters = lax.axis_size("blk")
    cluster = lax.axis_index("blk")
    gathered = lax.all_gather(drive_low, "rows", axis=1, tiled=True)
    column_blocks = gathered.shape[1] // tile_size
    row_blocks = panels // tile_size
    drive_blocks = gathered.reshape(excite_count, column_blocks, tile_size)
    load_blocks = loads_low.reshape(excite_count, row_blocks, tile_size)
    used_slots = tile_count[0]

    def near_group(group_index, carry):
        ahead, behind = carry
        first_slot = group_index * 4
        tile_group = lax.dynamic_slice_in_dim(near_tiles, first_slot, 4, 0)
        row_ids = lax.dynamic_slice_in_dim(tile_rows, first_slot, 4, 0)
        column_ids = lax.dynamic_slice_in_dim(tile_cols, first_slot, 4, 0)
        live_mask = (first_slot + jnp.arange(4, dtype=jnp.int32) < used_slots).astype(jnp.float32)[
            None, :, None
        ]
        source = jnp.take(drive_blocks, column_ids, axis=1)
        target = jnp.take(load_blocks, row_ids, axis=1)
        forward = (
            jnp.einsum("egj,gij->egi", source, tile_group, preferred_element_type=jnp.float32)
            * live_mask
        )
        backward = (
            jnp.einsum("egi,gij->egj", target, tile_group, preferred_element_type=jnp.float32)
            * live_mask
        )
        return (ahead.at[:, row_ids].add(forward), behind.at[:, column_ids].add(backward))

    near_start = (
        jnp.zeros((excite_count, row_blocks, tile_size), jnp.float32),
        jnp.zeros((excite_count, column_blocks, tile_size), jnp.float32),
    )
    near_ahead, near_behind = lax.fori_loop(0, (used_slots + 3) // 4, near_group, near_start)
    contract_panels = (((1,), (1,)), ((), ()))
    charge_part = lax.dot_general(
        drive_low, skeleton_in, contract_panels, preferred_element_type=jnp.float32
    )
    gradient_part = lax.dot_general(
        loads_low, skeleton_out, contract_panels, preferred_element_type=jnp.float32
    )
    charges, gradient_all = lax.psum((charge_part, gradient_part), "rows")
    gradient = lax.dynamic_slice_in_dim(
        gradient_all, lax.axis_index("rows") * share_width, share_width, 1
    )

    def offsets_for(other_ids):
        offset = jnp.remainder(cluster - other_ids, clusters)
        active = (offset != 0).astype(jnp.float32)
        return (jnp.maximum(offset - 1, 0), active)

    charge_piece = lax.all_gather(charges[None], "blk", axis=0, tiled=True)
    span_count = charge_piece.shape[0]
    offset, active = offsets_for(jnp.arange(span_count, dtype=jnp.int32))
    chosen = jnp.take(kernels, offset, axis=0)
    potential = jnp.einsum(
        "cej,ckj->ek", charge_piece * active[:, None, None], chosen, precision=highest
    )
    potential_low = lax.all_gather(potential.astype(jnp.bfloat16), "rows", axis=1, tiled=True)
    far_ahead = jnp.dot(potential_low, skeleton_out, preferred_element_type=jnp.float32)
    offset, active = offsets_for(jnp.arange(lax.axis_size("blk") * 1, dtype=jnp.int32))
    chosen = jnp.take(kernels, offset, axis=0)
    summed = lax.psum_scatter(
        jnp.einsum("ek,ckj->cej", gradient, chosen, precision=highest) * active[:, None, None],
        "blk",
        scatter_dimension=0,
        tiled=True,
    )
    adjoint_low = lax.psum(summed[0], "rows").astype(jnp.bfloat16)
    far_behind = jnp.dot(adjoint_low, skeleton_in, preferred_element_type=jnp.float32)
    near_columns = lax.psum_scatter(
        near_behind.reshape(excite_count, column_blocks * tile_size),
        "rows",
        scatter_dimension=1,
        tiled=True,
    )
    response = near_ahead.reshape(excite_count, panels) + far_ahead
    sensitivity = near_columns + far_behind
    return (response, sensitivity)


def solution(mesh):
    return jax.shard_map(
        on_device,
        mesh=mesh,
        in_specs=(
            P(None, ("blk", "rows")),
            P(None, ("blk", "rows")),
            P(("blk", "rows"), None, None),
            P(("blk", "rows")),
            P(("blk", "rows")),
            P(("blk", "rows")),
            P(None, ("blk", "rows")),
            P(None, ("blk", "rows")),
            P("blk", None, "rows", None),
        ),
        out_specs=(P(None, ("blk", "rows")), P(None, ("blk", "rows"))),
        check_vma=False,
    )
```

profile of v0, /device:TPU:0, one launch (start us, length us, event | category | flops | bytes accessed | tf_op | source)
XLA Modules:
  0.0 199.4 jit_solution(9917593990878031610)
XLA Ops:
  7.2 1.0 convert_element_type.27
  8.2 0.9 convert_element_type.28
  9.1 2.4 %fusion.45 = f32[64,1024]{1,0:T(8,128)} fusion(bf16[64,512]{1,0:T(8,128)(2,1)S(1)} %convert_element_type.28, bf16[1024,512]{1,0:T(8,128)(2,1)} %param.20), kind=kOutput, calls=%fused_computation.62 | convolution fusion | flops 67108864 | bytes 1376256 | tf_op jit(solution)/shard_map/dot_general | solution.py:66
  11.5 1.2 convolution_bitcast_fusion
  13.4 17.3 %all_gather.9 = bf16[64,2048]{1,0:T(8,128)(2,1)S(1)} all-gather(bf16[64,512]{1,0:T(8,128)(2,1)S(1)} %convert_element_type.27), channel_id=1, replica_groups=mesh['blk'=8,'rows'=4] {'rows'}, dimensions={1}, use_global_device_ids=true | all-gather | bytes 327680 | tf_op jit(solution)/shard_map/all_gather | solution.py:29
  30.8 7.4 %gather_fusion.2 = f32[8,256,1024]{2,1,0:T(8,128)} fusion(f32[7,256,1024]{2,1,0:T(8,128)} %bitcast.55, s32[1024]{0:T(1024)S(1)} %pad_clamp_fusion.2), kind=kCustom, calls=%fused_computation.2.clone | custom fusion | bytes 16777248 | tf_op jit(solution)/shard_map/jit(_take)/gather | solution.py:82
  38.2 17.6 %all-reduce.4.cloned.1.call-done = (f32[1,64,1024]{2,1,0:T(8,128)}, f32[64,1024]{1,0:T(8,128)}) async-done(((f32[1,64,1024]{2,1,0:T(8,128)}, f32[64,1024]{1,0:T(8,128)}), (f32[1,64,1024]{2,1,0:T(8,128)}, f32[64,1024]{1,0:T(8,128)})) %all-reduce.4.cloned.1.call-update) | async-done | bytes 524304 | tf_op jit(solution)/shard_map/psum | solution.py:69
  55.9 10.5 %multiply_bitcast_fusion = f32[8,64,1024]{2,1,0:T(8,128)} fusion(f32[8,256,1024]{2,1,0:T(8,128)} %gather_fusion.2, pred[8]{0:T(512)(128)(4,1)S(1)} %get-tuple-element.107, f32[8]{0:T(128)S(1)} %get-tuple-element.106, f32[64,1024]{1,0:T(8,128)} %get-tuple-element.100, s32[]{:T(128)S(6)} %select_n.53), kind=kOutput, calls=%fused_computation.38 | convolution fusion | flops 1613234176 | bytes 10551340 | tf_op jit(solution)/shard_map/ek,ckj->cej/dot_general | solution.py:91
  66.5 12.3 %while.12 = (s32[]{:T(128)}, f32[64,2,256]{2,0,1:T(8,128)S(1)}, f32[64,8,256]{2,0,1:T(8,128)S(1)}, s32[]{:T(128)}, s32[32]{0:T(128)S(1)}, /*index=5*/bf16[32,256...) while((s32[]{:T(128)}, f32[64,2,256]{2,0,1:T(8,128)S(1)}, ...), condition=%wide.region_3.4_spmd, body=%wide.region_0.3_spmd.sunk | while | flops 67504192 | bytes 3940779 | solution.py:61
  66.6 0.7 compare_and_fusion.4
  67.4 0.6 gather_fusion.1
  67.9 0.6 gather_fusion
  68.5 1.3 fusion.64
  69.8 0.8 scatter_fusion
  70.6 1.3 fusion.65
  71.9 0.7 scatter_fusion.1
  72.7 0.7 compare_and_fusion.4
  73.5 0.6 gather_fusion.1
  74.1 0.6 gather_fusion
  74.6 1.3 fusion.64
  76.0 0.7 scatter_fusion
  76.7 1.3 fusion.65
  78.1 0.8 scatter_fusion.1
  78.8 0.9 copy.28
  79.8 0.5 all-gather.2.cloned.1.call-update
  80.3 27.4 %reduce-scatter.5.cloned.1.call-done = f32[1,64,1024]{2,1,0:T(8,128)} async-done(((f32[8,64,1024]{2,1,0:T(8,128)}), f32[1,64,1024]{2,1,0:T(8,128)}) %reduce-scatter.5.cloned.1.call-update) | async-done | bytes 262160 | tf_op jit(solution)/shard_map/reduce_scatter | solution.py:90
  107.7 34.4 %all-reduce.5 = bf16[64,1024]{1,0:T(8,128)(2,1)S(1)} all-reduce(f32[64,1024]{1,0:T(8,128)} %bitcast.62), channel_id=1, replica_groups=mesh['blk'=8,'rows'=4] {'rows'}, use_global_device_ids=true, to_apply=%region_8.10 | all-reduce | flops 65536 | bytes 393216 | tf_op jit(solution)/shard_map/psum | solution.py:96
  142.2 1.9 convolution_add_fusion
  144.1 22.6 %all-gather.2.cloned.1.call-done = f32[8,64,1024]{2,1,0:T(8,128)} async-done(((f32[1,64,1024]{2,1,0:T(8,128)}), f32[8,64,1024]{2,1,0:T(8,128)}) %all-gather.2.cloned.1.call-update) | async-done | bytes 2097168 | tf_op jit(solution)/shard_map/all_gather | solution.py:79
  166.7 11.8 %fusion.32 = bf16[64,256]{1,0:T(8,128)(2,1)S(1)} fusion(f32[8,256,1024]{2,1,0:T(8,128)} %gather_fusion.2, pred[8]{0:T(512)(128)(4,1)S(1)} %get-tuple-element.107, f32[8,64,1024]{2,1,0:T(8,128)} %all-gather.2.cloned.1.call-done, f32[8]{0:T(128)S(1)} %get-tuple-element.106), kind=kOutput, calls=%fused_computation.44 | convolution fusion | flops 1613250560 | bytes 10518568 | tf_op jit(solution)/shard_map/cej,ckj->ek/dot_general | solution.py:83
  178.5 13.4 %all_gather.11 = bf16[64,1024]{1,0:T(8,128)(2,1)S(1)} all-gather(bf16[64,256]{1,0:T(8,128)(2,1)S(1)} %fusion.32), channel_id=1, replica_groups=mesh['blk'=8,'rows'=4] {'rows'}, dimensions={1}, use_global_device_ids=true | all-gather | bytes 163840 | tf_op jit(solution)/shard_map/all_gather | solution.py:86
  191.9 1.0 convolution_add_fusion.1
  (30 shorter events, 0.5 us)
Async XLA Ops:
  7.2 4.4 %copy-start = (bf16[1024,512]{1,0:T(8,128)(2,1)S(1)}, bf16[1024,512]{1,0:T(8,128)(2,1)}, u32[]{:S(2)}) copy-start(bf16[1024,512]{1,0:T(8,128)(2,1)} %param.19) | copy-start | bytes 3145732
  7.2 48.7 %all-reduce.4.cloned.1.call-start = ((), (), s32[]{:S(2)}) async-start(), calls=%async_computation.5 | async-start | bytes 1048576 | tf_op jit(solution)/shard_map/psum | solution.py:69
  12.7 95.0 %reduce-scatter.5.cloned.1.call-start = ((), (), s32[]{:S(2)}) async-start(), calls=%async_computation.4 | async-start | bytes 2359296 | tf_op jit(solution)/shard_map/reduce_scatter | solution.py:90
  55.9 10.7 %copy-start.2 = (s32[32]{0:T(128)S(1)}, s32[32]{0:T(128)}, u32[]{:S(2)}) copy-start(s32[32]{0:T(128)} %param.16) | copy-start | bytes 388
  55.9 10.7 %copy-start.3 = (s32[32]{0:T(128)S(1)}, s32[32]{0:T(128)}, u32[]{:S(2)}) copy-start(s32[32]{0:T(128)} %param.17) | copy-start | bytes 388
  66.4 75.8 %reduce-scatter.3.cloned.1.call-start = ((), (), s32[]{:S(2)}) async-start(), calls=%async_computation.3 | async-start | bytes 655360 | tf_op jit(solution)/shard_map/reduce_scatter | solution.py:98
  79.7 86.9 %all-gather.2.cloned.1.call-start = ((), (), s32[]{:S(2)}) async-start(), calls=%async_computation.2 | async-start | bytes 2359296 | tf_op jit(solution)/shard_map/all_gather | solution.py:79
  144.1 47.8 %copy-start.1 = (bf16[1024,512]{1,0:T(8,128)(2,1)S(1)}, bf16[1024,512]{1,0:T(8,128)(2,1)}, u32[]{:S(2)}) copy-start(bf16[1024,512]{1,0:T(8,128)(2,1)} %param.20) | copy-start | bytes 3145732
Sparse Core Ops, SparseCore 0:
  12.8 42.9 all-reduce.3
  66.5 41.1 reduce-scatter.4
  110.1 27.7 reduce-scatter.2
  139.8 26.8 all-gather.1
where the time goes:
time: 200 us; the launch traced here: 199 us
  waiting for transfers between devices  68.2 us (34%)
  blocking collectives  65.1 us (33%)
  matrix products  34 us (17%)
  between operations  14.6 us (7%)
  local copies, waits for them, and re-layouts  10.6 us (5%)
  other arithmetic  6.58 us (3%)
    psum x1, blocking collectives, on_device(): adjoint_low = lax.psum(summed[0], 'rows').astype(jnp.bfloat16)  34.4 us
    reduce_scatter x1, waiting for transfers between devices, on_device(): lax.psum_scatter(jnp.einsum('ek,ckj->cej', gradient, chosen, precision=hi...  27.4 us
    all_gather x1, waiting for transfers between devices, on_device(): charge_piece = lax.all_gather(charges[None], 'blk', axis=0, tiled=True)  22.6 us
    psum x1, waiting for transfers between devices, on_device(): charges, gradient_all = lax.psum((charge_part, gradient_part), 'rows')  17.6 us
    all_gather x1, blocking collectives, on_device(): gathered = lax.all_gather(drive_low, 'rows', axis=1, tiled=True)  17.3 us
    all_gather x1, blocking collectives, on_device(): lax.all_gather(potential.astype(jnp.bfloat16), 'rows', axis=1, tiled=True)  13.4 us
    dot_general x1, matrix products, on_device(): jnp.einsum('cej,ckj->ek', charge_piece * active[:, None, None], chosen, p...  11.8 us
    dot_general x1, matrix products, on_device(): jnp.einsum('ek,ckj->cej', gradient, chosen, precision=highest)  10.5 us
  transfers between devices with their start and end apart: 4, of which 3 were waited for; matrix products, arithmetic and copies ran while one was open for 11% of the time, Pallas kernels for 0%

commit v1 on v0

--- a/solution.py
+++ b/solution.py
@@ -1,12 +1,16 @@
+import functools
+
 import jax
 import jax.numpy as jnp
 from jax import lax
+from jax.experimental import pallas as pl
+from jax.experimental.pallas import tpu as pltpu
 from jax.sharding import PartitionSpec as P
 
 highest = lax.Precision.HIGHEST
 
 
-def on_device(
+def plain_plan(
     excitations,
     adjoint_loads,
     near_tiles,
@@ -106,7 +110,447 @@
     return (response, sensitivity)
 
 
+MESH = pl.DeviceIdType.MESH
+GROUP = 4
+bf16 = jnp.bfloat16
+f32 = jnp.float32
+
+
+def dot_nt(a, b):
+    return lax.dot_general(a, b, (((1,), (1,)), ((), ())), preferred_element_type=f32)
+
+
+def dot_nn(a, b):
+    return jnp.dot(a, b, preferred_element_type=f32)
+
+
+def kernel(
+    rows,
+    clusters,
+    count_ref,
+    tile_row_ref,
+    tile_col_ref,
+    drive_ref,
+    loads_ref,
+    tiles_hbm,
+    skin_hbm,
+    skout_hbm,
+    trans_hbm,
+    response_ref,
+    sensitivity_ref,
+    tiles,
+    skin,
+    skout,
+    trans,
+    trans_low,
+    drive_all,
+    loads_low,
+    grad_part,
+    grad_send,
+    grad_recv,
+    charge_part,
+    charge_send,
+    charge_recv,
+    q_all,
+    sib_send,
+    sib_recv,
+    plane_send,
+    plane_recv,
+    adj_part,
+    adj_send,
+    adj_recv,
+    adj_all,
+    pot_all,
+    near_fwd,
+    near_adj,
+    near_send,
+    near_recv,
+    local_sem,
+    send_sem,
+    grad_sem,
+    charge_sem,
+    drive_sem,
+    qz_sem,
+    qp_sem,
+    qs_sem,
+    sib_sem,
+    plane_sem,
+    adj_sem,
+    adjall_sem,
+    pot_sem,
+    near_sem,
+):
+    chips = clusters // 2
+    b = lax.axis_index("blk")
+    r = lax.axis_index("rows")
+    core = lax.rem(b, 2)
+    chip = lax.div(b, 2)
+    cap, size = tiles.shape[0], tiles.shape[1]
+    share = q_all.shape[3]
+    row_blocks = loads_low.shape[0]
+    column_blocks = rows * row_blocks
+    offsets = trans.shape[0]
+
+    def row_at(step):
+        return lax.rem(r + step + rows, rows)
+
+    def blk_at(step, which):
+        return lax.rem(chip + step + chips, chips) * 2 + which
+
+    sibling = b + 1 - 2 * core
+
+    local = []
+
+    def fetch(src, dst):
+        copy = pltpu.make_async_copy(src, dst, local_sem.at[len(local)])
+        copy.start()
+        local.append(copy)
+        return copy
+
+    get_out = fetch(skout_hbm, skout)
+    get_in = fetch(skin_hbm, skin)
+    get_trans = [fetch(trans_hbm.at[d], trans.at[d]) for d in range(offsets)]
+    get_tiles = fetch(tiles_hbm, tiles)
+
+    sent = []
+
+    def send(src, dst, recv, blk, row):
+        copy = pltpu.make_async_remote_copy(
+            src_ref=src,
+            dst_ref=dst,
+            send_sem=send_sem.at[len(sent)],
+            recv_sem=recv,
+            device_id=(blk, row),
+            device_id_type=MESH,
+        )
+        copy.start()
+        sent.append(copy)
+        return copy
+
+    barrier = pltpu.get_barrier_semaphore()
+    partners = [(b, row_at(o)) for o in range(1, rows)]
+    partners += [(blk_at(o, core), r) for o in range(1, chips)]
+    partners += [(sibling, r)]
+    for partner in partners:
+        pl.semaphore_signal(barrier, inc=1, device_id=partner, device_id_type=MESH)
+
+    for i in range(row_blocks):
+        loads_low[i] = loads_ref[:, i * size : (i + 1) * size].astype(bf16)
+        drive_all[r * row_blocks + i] = drive_ref[:, i * size : (i + 1) * size].astype(bf16)
+    loads_wide = loads_ref[...].astype(bf16)
+    get_out.wait()
+    for j in range(rows):
+        part = dot_nt(loads_wide, skout[j * share : (j + 1) * share, :])
+        grad_part[j] = part
+        grad_send[j] = part.astype(bf16)
+    pl.semaphore_wait(barrier, len(partners))
+    grad_copies = [
+        send(grad_send.at[row_at(o)], grad_recv.at[o - 1], grad_sem.at[o - 1], b, row_at(o))
+        for o in range(1, rows)
+    ]
+    drive_wide = drive_ref[...].astype(bf16)
+    get_in.wait()
+    for j in range(rows):
+        part = dot_nt(drive_wide, skin[j * share : (j + 1) * share, :])
+        charge_part[j] = part
+        charge_send[j] = part.astype(bf16)
+    charge_copies = [
+        send(charge_send.at[row_at(o)], charge_recv.at[o - 1], charge_sem.at[o - 1], b, row_at(o))
+        for o in range(1, rows)
+    ]
+    mine = pl.ds(r * row_blocks, row_blocks)
+    drive_copies = [
+        send(drive_all.at[mine], drive_all.at[mine], drive_sem.at[o - 1], b, row_at(o))
+        for o in range(1, rows)
+    ]
+
+    for d in range(offsets):
+        get_trans[d].wait()
+        trans_low[d] = trans[d].astype(bf16)
+
+    for copy in grad_copies:
+        copy.wait_recv()
+    gradient = grad_part[r]
+    for o in range(rows - 1):
+        gradient += grad_recv[o].astype(f32)
+    grad_high = gradient.astype(bf16)
+    grad_rest = (gradient - grad_high.astype(f32)).astype(bf16)
+    grad_both = jnp.concatenate([grad_high, grad_rest], axis=0)
+    excite = gradient.shape[0]
+
+    for copy in charge_copies:
+        copy.wait_recv()
+    charge = charge_part[r]
+    for o in range(rows - 1):
+        charge += charge_recv[o].astype(f32)
+    q_all[r, b] = charge.astype(bf16)
+
+    def send_quarter_to_plane(z):
+        piece = q_all.at[row_at(-z), b]
+        copies = [
+            send(piece, piece, qp_sem.at[z, o - 1], blk_at(o, core), r) for o in range(1, chips)
+        ]
+        return copies, [send(piece, piece, qs_sem.at[z, 0], sibling, r)]
+
+    piece = q_all.at[r, b]
+    qz_copies = [send(piece, piece, qz_sem.at[o - 1], b, row_at(o)) for o in range(1, rows)]
+    plane_q, sibling_q = [None] * rows, [None] * rows
+    plane_q[0], sibling_q[0] = send_quarter_to_plane(0)
+
+    def adjoint_term(target, j):
+        index = lax.rem(b - target + clusters, clusters) - 1
+        both = dot_nn(grad_both, trans_low[index, :, j * share : (j + 1) * share])
+        return both[:excite] + both[excite:]
+
+    sib_copies = []
+    for o in range(chips):
+        for j in range(rows):
+            sib_send[o, j] = adjoint_term(blk_at(o, 1 - core), j).astype(bf16)
+        sib_copies.append(send(sib_send.at[o], sib_recv.at[o], sib_sem.at[o], sibling, r))
+    for z in range(1, rows):
+        qz_copies[z - 1].wait_recv()
+        plane_q[z], sibling_q[z] = send_quarter_to_plane(z)
+    plane_copies = []
+    for o in range(1, chips):
+        terms = [adjoint_term(blk_at(o, core), j) for j in range(rows)]
+        sib_copies[o].wait_recv()
+        for j in range(rows):
+            plane_send[o - 1, j] = (terms[j] + sib_recv[o, j].astype(f32)).astype(bf16)
+        plane_copies.append(
+            send(
+                plane_send.at[o - 1],
+                plane_recv.at[o - 1],
+                plane_sem.at[o - 1],
+                blk_at(o, core),
+                r,
+            )
+        )
+
+    used = count_ref[0]
+    near_adj[...] = jnp.zeros_like(near_adj)
+    near_fwd[...] = jnp.zeros_like(near_fwd)
+    get_tiles.wait()
+
+    def adjoint_group(group, carry):
+        products, columns = [], []
+        for t in range(GROUP):
+            slot = group * GROUP + t
+            source = loads_low[tile_row_ref[slot]]
+            products.append(dot_nn(source, tiles[slot]))
+            columns.append(jnp.where(slot < used, tile_col_ref[slot], -1))
+        for c in range(column_blocks):
+            total = near_adj[c]
+            for t in range(GROUP):
+                total += products[t] * jnp.where(columns[t] == c, 1.0, 0.0).astype(f32)
+            near_adj[c] = total
+        return carry
+
+    def forward_group(group, carry):
+        products, targets = [], []
+        for t in range(GROUP):
+            slot = group * GROUP + t
+            source = drive_all[tile_col_ref[slot]]
+            products.append(dot_nt(source, tiles[slot]))
+            targets.append(jnp.where(slot < used, tile_row_ref[slot], -1))
+        for i in range(row_blocks):
+            total = near_fwd[i]
+            for t in range(GROUP):
+                total += products[t] * jnp.where(targets[t] == i, 1.0, 0.0).astype(f32)
+            near_fwd[i] = total
+        return carry
+
+    groups = cap // GROUP
+    lax.fori_loop(0, groups, adjoint_group, 0)
+    for c in range(column_blocks):
+        near_send[c] = near_adj[c].astype(bf16)
+    near_copies = [
+        send(
+            near_send.at[pl.ds(row_at(o) * row_blocks, row_blocks)],
+            near_recv.at[o - 1],
+            near_sem.at[o - 1],
+            b,
+            row_at(o),
+        )
+        for o in range(1, rows)
+    ]
+
+    for z in range(rows):
+        for o in range(1, chips):
+            plane_q[z][o - 1].wait_recv()
+            piece = q_all.at[row_at(-z), blk_at(-o, core)]
+            sibling_q[z].append(send(piece, piece, qs_sem.at[z, o], sibling, r))
+
+    for copy in drive_copies:
+        copy.wait_recv()
+    lax.fori_loop(0, groups // 2, forward_group, 0)
+
+    sib_copies[0].wait_recv()
+    for copy in plane_copies:
+        copy.wait_recv()
+    for j in range(rows):
+        total = sib_recv[0, j].astype(f32)
+        for o in range(chips - 1):
+            total += plane_recv[o, j].astype(f32)
+        adj_part[j] = total
+        adj_send[j] = total.astype(bf16)
+    adj_copies = [
+        send(adj_send.at[row_at(o)], adj_recv.at[o - 1], adj_sem.at[o - 1], b, row_at(o))
+        for o in range(1, rows)
+    ]
+
+    lax.fori_loop(groups // 2, groups, forward_group, 0)
+
+    for z in range(rows):
+        for copy in sibling_q[z]:
+            copy.wait_recv()
+    potential = jnp.zeros((excite, share), f32)
+    for j in range(rows):
+        for d in range(1, offsets + 1):
+            source = q_all[j, lax.rem(b - d + clusters, clusters)]
+            potential += dot_nt(source, trans_low[d - 1, :, j * share : (j + 1) * share])
+    pot_all[r] = potential.astype(bf16)
+    piece = pot_all.at[r]
+    pot_copies = [send(piece, piece, pot_sem.at[o - 1], b, row_at(o)) for o in range(1, rows)]
+
+    for copy in adj_copies:
+        copy.wait_recv()
+    adjoint = adj_part[r]
+    for o in range(rows - 1):
+        adjoint += adj_recv[o].astype(f32)
+    adj_all[r] = adjoint.astype(bf16)
+    piece = adj_all.at[r]
+    adjall_copies = [send(piece, piece, adjall_sem.at[o - 1], b, row_at(o)) for o in range(1, rows)]
+
+    for copy in near_copies:
+        copy.wait_recv()
+    for i in range(row_blocks):
+        total = near_adj[r * row_blocks + i]
+        for o in range(rows - 1):
+            total += near_recv[o, i].astype(f32)
+        near_adj[r * row_blocks + i] = total
+
+    for copy in pot_copies:
+        copy.wait_recv()
+    for i in range(row_blocks):
+        total = near_fwd[i]
+        for j in range(rows):
+            block = skout[j * share : (j + 1) * share, i * size : (i + 1) * size]
+            total += dot_nn(pot_all[j], block)
+        response_ref[:, i * size : (i + 1) * size] = total
+    for copy in adjall_copies:
+        copy.wait_recv()
+    for i in range(row_blocks):
+        total = near_adj[r * row_blocks + i]
+        for j in range(rows):
+            block = skin[j * share : (j + 1) * share, i * size : (i + 1) * size]
+            total += dot_nn(adj_all[j], block)
+        sensitivity_ref[:, i * size : (i + 1) * size] = total
+    for copy in sent:
+        copy.wait_send()
+
+
+def fused_plan(
+    rows,
+    clusters,
+    excitations,
+    adjoint_loads,
+    near_tiles,
+    tile_rows,
+    tile_cols,
+    tile_count,
+    skeleton_in,
+    skeleton_out,
+    translation,
+):
+    kernels = translation[0]
+    excite, panels = excitations.shape
+    cap, size = near_tiles.shape[:2]
+    offsets, share, points = kernels.shape
+    chips = clusters // 2
+    row_blocks = panels // size
+    blocks = rows * row_blocks
+    others = rows - 1
+    sends = 7 * others + rows * (chips - 1) + rows * chips + chips + chips - 1 + others
+    vmem, dma = pltpu.VMEM, pltpu.SemaphoreType.DMA
+    scratch = [
+        vmem((cap, size, size), bf16),
+        vmem((points, panels), bf16),
+        vmem((points, panels), bf16),
+        vmem((offsets, share, points), f32),
+        vmem((offsets, share, points), bf16),
+        vmem((blocks, excite, size), bf16),
+        vmem((row_blocks, excite, size), bf16),
+        vmem((rows, excite, share), f32),
+        vmem((rows, excite, share), bf16),
+        vmem((others, excite, share), bf16),
+        vmem((rows, excite, share), f32),
+        vmem((rows, excite, share), bf16),
+        vmem((others, excite, share), bf16),
+        vmem((rows, clusters, excite, share), bf16),
+        vmem((chips, rows, excite, share), bf16),
+        vmem((chips, rows, excite, share), bf16),
+        vmem((chips - 1, rows, excite, share), bf16),
+        vmem((chips - 1, rows, excite, share), bf16),
+        vmem((rows, excite, share), f32),
+        vmem((rows, excite, share), bf16),
+        vmem((others, excite, share), bf16),
+        vmem((rows, excite, share), bf16),
+        vmem((rows, excite, share), bf16),
+        vmem((row_blocks, excite, size), f32),
+        vmem((blocks, excite, size), f32),
+        vmem((blocks, excite, size), bf16),
+        vmem((others, row_blocks, excite, size), bf16),
+        dma((offsets + 3,)),
+        dma((sends,)),
+        dma((others,)),
+        dma((others,)),
+        dma((others,)),
+        dma((others,)),
+        dma((rows, chips - 1)),
+        dma((rows, chips)),
+        dma((chips,)),
+        dma((chips - 1,)),
+        dma((others,)),
+        dma((others,)),
+        dma((others,)),
+        dma((others,)),
+    ]
+    whole_vmem = pl.BlockSpec(memory_space=pltpu.VMEM)
+    whole_smem = pl.BlockSpec(memory_space=pltpu.SMEM)
+    anywhere = pl.BlockSpec(memory_space=pl.ANY)
+    return pl.pallas_call(
+        functools.partial(kernel, rows, clusters),
+        out_shape=[jax.ShapeDtypeStruct((excite, panels), f32)] * 2,
+        in_specs=[whole_smem] * 3 + [whole_vmem] * 2 + [anywhere] * 4,
+        out_specs=[whole_vmem] * 2,
+        scratch_shapes=scratch,
+        compiler_params=pltpu.CompilerParams(
+            collective_id=0, has_side_effects=True, vmem_limit_bytes=48 * 1024 * 1024
+        ),
+    )(
+        tile_count,
+        tile_rows,
+        tile_cols,
+        excitations,
+        adjoint_loads,
+        near_tiles,
+        skeleton_in,
+        skeleton_out,
+        kernels,
+    )
+
+
 def solution(mesh):
+    clusters, rows = mesh.shape["blk"], mesh.shape["rows"]
+
+    def on_device(*args):
+        share = args[8].shape[2]
+        tile_size = args[2].shape[1]
+        fits = clusters == 8 and rows == 4 and share % 128 == 0
+        if fits and tile_size % 128 == 0 and args[2].shape[0] % (2 * GROUP) == 0:
+            return tuple(fused_plan(rows, clusters, *args))
+        return plain_plan(*args)
+
     return jax.shard_map(
         on_device,
         mesh=mesh,

time: 200 us -> 50.5 us (0.25)
  waiting for transfers between devices: 68.2 us -> 0 us
  blocking collectives: 65.1 us -> 0 us
  Pallas kernels: 0 us -> 42.1 us
  matrix products: 34 us -> 0 us
  between operations: 14.6 us -> 1.3 us
  other arithmetic: 6.58 us -> 0 us
  local copies, waits for them, and re-layouts: 10.6 us -> 6.87 us
    pallas_call x0 -> x1, Pallas kernels: none -> 42.1 us  [fused_plan(): pl.pallas_call(functools.partial(kernel, rows, clusters), out_shape=[jax....]
    psum x1 -> x0, blocking collectives: 34.4 us -> none  [on_device(): adjoint_low = lax.psum(summed[0], 'rows').astype(jnp.bfloat16)]
    dot_general x10 -> x0, matrix products: 34 us -> none  [the longest x1 11.8 us: on_device(): jnp.einsum('cej,ckj->ek', charge_piece * active[:, None, None], chosen, p...]
    all_gather x2 -> x0, blocking collectives: 30.7 us -> none  [the longest x1 17.3 us: on_device(): gathered = lax.all_gather(drive_low, 'rows', axis=1, tiled=True)]
    reduce_scatter x2 -> x0, waiting for transfers between devices: 27.4 us -> none  [the longest x1 27.4 us: on_device(): lax.psum_scatter(jnp.einsum('ek,ckj->cej', gradient, chosen, precision=hi...]
    all_gather x1 -> x0, waiting for transfers between devices: 22.6 us -> none  [on_device(): charge_piece = lax.all_gather(charges[None], 'blk', axis=0, tiled=True)]
    psum x1 -> x0, waiting for transfers between devices: 17.6 us -> none  [on_device(): charges, gradient_all = lax.psum((charge_part, gradient_part), 'rows')]
    gather x5 -> x0, local copies, waits for them, and re-layouts: 9.63 us -> none  [the longest x1 7.41 us: on_device(): chosen = jnp.take(kernels, offset, axis=0)]
  transfers between devices with their start and end apart: 4 -> 0, of which waited for: 3 -> 0; matrix products, arithmetic and copies ran while one was open for 11% -> 0% of each run, Pallas kernels for 0% -> 0%
where the time goes in v1:
time: 50.5 us; the launch traced here: 50.3 us
  Pallas kernels  42.1 us (83%)
  local copies, waits for them, and re-layouts  6.87 us (14%)
  between operations  1.3 us (3%)
    pallas_call x1, Pallas kernels, fused_plan(): pl.pallas_call(functools.partial(kernel, rows, clusters), out_shape=[jax....  42.1 us
    unnamed x14, local copies, waits for them, and re-layouts  6.87 us

profile of v1, /device:TPU:0, one launch (start us, length us, event | category | flops | bytes accessed | tf_op | source)
XLA Modules:
  0.0 50.3 jit_solution(15046075829485450928)
XLA Ops:
  1.3 0.0 copy-start
  1.3 1.2 %copy-done = bf16[1024,512]{1,0:T(8,128)(2,1)S(1)} copy-done((bf16[1024,512]{1,0:T(8,128)(2,1)S(1)}, bf16[1024,512]{1,0:T(8,128)(2,1)}, u32[]{:S(2)}) %copy-start) | copy-done | bytes 1048600
  2.5 0.0 copy-start.1
  2.5 1.2 %copy-done.1 = bf16[1024,512]{1,0:T(8,128)(2,1)S(1)} copy-done((bf16[1024,512]{1,0:T(8,128)(2,1)S(1)}, bf16[1024,512]{1,0:T(8,128)(2,1)}, u32[]{:S(2)}) %copy-start.1) | copy-done | bytes 1048600
  3.7 0.0 copy-start.2
  3.7 0.9 %copy-done.2 = f32[64,512]{1,0:T(8,128)S(1)} copy-done((f32[64,512]{1,0:T(8,128)S(1)}, f32[64,512]{1,0:T(8,128)}, u32[]{:S(2)}) %copy-start.2) | copy-done | bytes 131096
  4.6 0.0 copy-start.3
  4.6 0.9 %copy-done.3 = f32[64,512]{1,0:T(8,128)S(1)} copy-done((f32[64,512]{1,0:T(8,128)S(1)}, f32[64,512]{1,0:T(8,128)}, u32[]{:S(2)}) %copy-start.3) | copy-done | bytes 131096
  5.5 0.0 copy-start.4
  5.5 0.7 %copy-done.4 = s32[32]{0:T(128)S(1)} copy-done((s32[32]{0:T(128)S(1)}, s32[32]{0:T(128)}, u32[]{:S(2)}) %copy-start.4) | copy-done | bytes 152
  6.2 0.0 copy-start.5
  6.2 0.7 %copy-done.5 = s32[32]{0:T(128)S(1)} copy-done((s32[32]{0:T(128)S(1)}, s32[32]{0:T(128)}, u32[]{:S(2)}) %copy-start.5) | copy-done | bytes 152
  6.9 42.1 %shard_map.104 = (f32[64,512]{1,0:T(8,128)S(1)}, f32[64,512]{1,0:T(8,128)S(1)}) custom-call(s32[1]{0:T(128)S(6)} %copy.13.count_ref, s32[32]{0:T(128)S(1)} %copy-done.4, s32[32]{0:T(128)S(1)} %copy-done.5, f32[64,512]{1,0:T(8,128)S(1)} %copy-done.2, f32[64,512]{1,0:T(8,128)S(1)} %copy-done.3, bf16[32,256,256]{2,1,0:T(8,128)(2,1)} %tiles_hbm.1, ...), custom_call_target="tpu_custom_call" | custom-call | tf_op jit(solution)/shard_map/pallas_call | solution.py:521
  48.9 0.7 %copy.14 = f32[64,512]{1,0:T(8,128)} copy(f32[64,512]{1,0:T(8,128)S(1)} %get-tuple-element.4) | data formatting | bytes 262144
  49.6 0.7 %copy.15 = f32[64,512]{1,0:T(8,128)} copy(f32[64,512]{1,0:T(8,128)S(1)} %get-tuple-element.5) | data formatting | bytes 262144
Async XLA Ops:
  1.3 1.2 %copy-start = (bf16[1024,512]{1,0:T(8,128)(2,1)S(1)}, bf16[1024,512]{1,0:T(8,128)(2,1)}, u32[]{:S(2)}) copy-start(bf16[1024,512]{1,0:T(8,128)(2,1)} %skin_hbm.1) | copy-start | bytes 3145732
  2.5 1.2 %copy-start.1 = (bf16[1024,512]{1,0:T(8,128)(2,1)S(1)}, bf16[1024,512]{1,0:T(8,128)(2,1)}, u32[]{:S(2)}) copy-start(bf16[1024,512]{1,0:T(8,128)(2,1)} %skout_hbm.1) | copy-start | bytes 3145732
  3.7 0.9 %copy-start.2 = (f32[64,512]{1,0:T(8,128)S(1)}, f32[64,512]{1,0:T(8,128)}, u32[]{:S(2)}) copy-start(f32[64,512]{1,0:T(8,128)} %drive_ref.1) | copy-start | bytes 393220
  4.6 0.9 %copy-start.3 = (f32[64,512]{1,0:T(8,128)S(1)}, f32[64,512]{1,0:T(8,128)}, u32[]{:S(2)}) copy-start(f32[64,512]{1,0:T(8,128)} %loads_ref.1) | copy-start | bytes 393220
  5.5 0.7 %copy-start.4 = (s32[32]{0:T(128)S(1)}, s32[32]{0:T(128)}, u32[]{:S(2)}) copy-start(s32[32]{0:T(128)} %tile_row_ref.1) | copy-start | bytes 388
  6.2 0.7 %copy-start.5 = (s32[32]{0:T(128)S(1)}, s32[32]{0:T(128)}, u32[]{:S(2)}) copy-start(s32[32]{0:T(128)} %tile_col_ref.1) | copy-start | bytes 388

commit v2 on v1

--- a/solution.py
+++ b/solution.py
@@ -112,6 +112,7 @@
 
 MESH = pl.DeviceIdType.MESH
 GROUP = 4
+VMEM_BYTES = 62 * 1024 * 1024
 bf16 = jnp.bfloat16
 f32 = jnp.float32
 
@@ -128,16 +129,20 @@
     rows,
     clusters,
     count_ref,
-    tile_row_ref,
-    tile_col_ref,
-    drive_ref,
-    loads_ref,
+    tile_row_hbm,
+    tile_col_hbm,
+    drive_hbm,
+    loads_hbm,
     tiles_hbm,
     skin_hbm,
     skout_hbm,
     trans_hbm,
     response_ref,
     sensitivity_ref,
+    tile_row_ref,
+    tile_col_ref,
+    drive_ref,
+    loads_ref,
     tiles,
     skin,
     skout,
@@ -207,10 +212,16 @@
         local.append(copy)
         return copy
 
+    get_loads = fetch(loads_hbm, loads_ref)
     get_out = fetch(skout_hbm, skout)
+    get_drive = fetch(drive_hbm, drive_ref)
     get_in = fetch(skin_hbm, skin)
     get_trans = [fetch(trans_hbm.at[d], trans.at[d]) for d in range(offsets)]
     get_tiles = fetch(tiles_hbm, tiles)
+    get_lists = [
+        fetch(tile_row_hbm, tile_row_ref),
+        fetch(tile_col_hbm, tile_col_ref),
+    ]
 
     sent = []
 
@@ -234,9 +245,9 @@
     for partner in partners:
         pl.semaphore_signal(barrier, inc=1, device_id=partner, device_id_type=MESH)
 
+    get_loads.wait()
     for i in range(row_blocks):
         loads_low[i] = loads_ref[:, i * size : (i + 1) * size].astype(bf16)
-        drive_all[r * row_blocks + i] = drive_ref[:, i * size : (i + 1) * size].astype(bf16)
     loads_wide = loads_ref[...].astype(bf16)
     get_out.wait()
     for j in range(rows):
@@ -248,6 +259,9 @@
         send(grad_send.at[row_at(o)], grad_recv.at[o - 1], grad_sem.at[o - 1], b, row_at(o))
         for o in range(1, rows)
     ]
+    get_drive.wait()
+    for i in range(row_blocks):
+        drive_all[r * row_blocks + i] = drive_ref[:, i * size : (i + 1) * size].astype(bf16)
     drive_wide = drive_ref[...].astype(bf16)
     get_in.wait()
     for j in range(rows):
@@ -258,11 +272,6 @@
         send(charge_send.at[row_at(o)], charge_recv.at[o - 1], charge_sem.at[o - 1], b, row_at(o))
         for o in range(1, rows)
     ]
-    mine = pl.ds(r * row_blocks, row_blocks)
-    drive_copies = [
-        send(drive_all.at[mine], drive_all.at[mine], drive_sem.at[o - 1], b, row_at(o))
-        for o in range(1, rows)
-    ]
 
     for d in range(offsets):
         get_trans[d].wait()
@@ -296,6 +305,12 @@
     qz_copies = [send(piece, piece, qz_sem.at[o - 1], b, row_at(o)) for o in range(1, rows)]
     plane_q, sibling_q = [None] * rows, [None] * rows
     plane_q[0], sibling_q[0] = send_quarter_to_plane(0)
+
+    mine = pl.ds(r * row_blocks, row_blocks)
+    drive_copies = [
+        send(drive_all.at[mine], drive_all.at[mine], drive_sem.at[o - 1], b, row_at(o))
+        for o in range(1, rows)
+    ]
 
     def adjoint_term(target, j):
         index = lax.rem(b - target + clusters, clusters) - 1
@@ -326,10 +341,13 @@
             )
         )
 
-    used = count_ref[0]
     near_adj[...] = jnp.zeros_like(near_adj)
     near_fwd[...] = jnp.zeros_like(near_fwd)
     get_tiles.wait()
+    for copy in get_lists:
+        copy.wait()
+
+    used = count_ref[0]
 
     def adjoint_group(group, carry):
         products, columns = [], []
@@ -382,23 +400,7 @@
 
     for copy in drive_copies:
         copy.wait_recv()
-    lax.fori_loop(0, groups // 2, forward_group, 0)
-
-    sib_copies[0].wait_recv()
-    for copy in plane_copies:
-        copy.wait_recv()
-    for j in range(rows):
-        total = sib_recv[0, j].astype(f32)
-        for o in range(chips - 1):
-            total += plane_recv[o, j].astype(f32)
-        adj_part[j] = total
-        adj_send[j] = total.astype(bf16)
-    adj_copies = [
-        send(adj_send.at[row_at(o)], adj_recv.at[o - 1], adj_sem.at[o - 1], b, row_at(o))
-        for o in range(1, rows)
-    ]
-
-    lax.fori_loop(groups // 2, groups, forward_group, 0)
+    lax.fori_loop(0, groups // 4, forward_group, 0)
 
     for z in range(rows):
         for copy in sibling_q[z]:
@@ -412,6 +414,22 @@
     piece = pot_all.at[r]
     pot_copies = [send(piece, piece, pot_sem.at[o - 1], b, row_at(o)) for o in range(1, rows)]
 
+    sib_copies[0].wait_recv()
+    for copy in plane_copies:
+        copy.wait_recv()
+    for j in range(rows):
+        total = sib_recv[0, j].astype(f32)
+        for o in range(chips - 1):
+            total += plane_recv[o, j].astype(f32)
+        adj_part[j] = total
+        adj_send[j] = total.astype(bf16)
+    adj_copies = [
+        send(adj_send.at[row_at(o)], adj_recv.at[o - 1], adj_sem.at[o - 1], b, row_at(o))
+        for o in range(1, rows)
+    ]
+
+    lax.fori_loop(groups // 4, groups // 4 * 3, forward_group, 0)
+
     for copy in adj_copies:
         copy.wait_recv()
     adjoint = adj_part[r]
@@ -420,6 +438,8 @@
     adj_all[r] = adjoint.astype(bf16)
     piece = adj_all.at[r]
     adjall_copies = [send(piece, piece, adjall_sem.at[o - 1], b, row_at(o)) for o in range(1, rows)]
+
+    lax.fori_loop(groups // 4 * 3, groups, forward_group, 0)
 
     for copy in near_copies:
         copy.wait_recv()
@@ -473,6 +493,10 @@
     sends = 7 * others + rows * (chips - 1) + rows * chips + chips + chips - 1 + others
     vmem, dma = pltpu.VMEM, pltpu.SemaphoreType.DMA
     scratch = [
+        pltpu.SMEM(tile_rows.shape, jnp.int32),
+        pltpu.SMEM(tile_cols.shape, jnp.int32),
+        vmem((excite, panels), f32),
+        vmem((excite, panels), f32),
         vmem((cap, size, size), bf16),
         vmem((points, panels), bf16),
         vmem((points, panels), bf16),
@@ -500,7 +524,7 @@
         vmem((blocks, excite, size), f32),
         vmem((blocks, excite, size), bf16),
         vmem((others, row_blocks, excite, size), bf16),
-        dma((offsets + 3,)),
+        dma((offsets + 7,)),
         dma((sends,)),
         dma((others,)),
         dma((others,)),
@@ -516,16 +540,15 @@
         dma((others,)),
     ]
     whole_vmem = pl.BlockSpec(memory_space=pltpu.VMEM)
-    whole_smem = pl.BlockSpec(memory_space=pltpu.SMEM)
     anywhere = pl.BlockSpec(memory_space=pl.ANY)
     return pl.pallas_call(
         functools.partial(kernel, rows, clusters),
         out_shape=[jax.ShapeDtypeStruct((excite, panels), f32)] * 2,
-        in_specs=[whole_smem] * 3 + [whole_vmem] * 2 + [anywhere] * 4,
+        in_specs=[pl.BlockSpec(memory_space=pltpu.SMEM)] + [anywhere] * 8,
         out_specs=[whole_vmem] * 2,
         scratch_shapes=scratch,
         compiler_params=pltpu.CompilerParams(
-            collective_id=0, has_side_effects=True, vmem_limit_bytes=48 * 1024 * 1024
+            collective_id=0, has_side_effects=True, vmem_limit_bytes=VMEM_BYTES
         ),
     )(
         tile_count,

time: 50.5 us -> 44.5 us (0.88)
  local copies, waits for them, and re-layouts: 6.87 us -> 3.14 us
  Pallas kernels: 42.1 us -> 39.9 us
    unnamed x14 -> x2, local copies, waits for them, and re-layouts: 6.87 us -> 3.14 us
    pallas_call x1, Pallas kernels: 42.1 us -> 39.9 us  [fused_plan(): pl.pallas_call(functools.partial(kernel, rows, clusters), out_shape=[jax....]
where the time goes in v2:
time: 44.5 us; the launch traced here: 44.4 us
  Pallas kernels  39.9 us (90%)
  local copies, waits for them, and re-layouts  3.14 us (7%)
  between operations  1.29 us (3%)
    pallas_call x1, Pallas kernels, fused_plan(): pl.pallas_call(functools.partial(kernel, rows, clusters), out_shape=[jax....  39.9 us
    unnamed x2, local copies, waits for them, and re-layouts  3.14 us

profile of v2, /device:TPU:0, one launch (start us, length us, event | category | flops | bytes accessed | tf_op | source)
XLA Modules:
  0.0 44.4 jit_solution(8285990487423727948)
XLA Ops:
  1.3 39.9 %shard_map.104 = (f32[64,512]{1,0:T(8,128)}, f32[64,512]{1,0:T(8,128)}) custom-call(s32[1]{0:T(128)S(6)} %copy.13.count_ref, s32[32]{0:T(128)} %tile_row_hbm.1, s32[32]{0:T(128)} %tile_col_hbm.1, f32[64,512]{1,0:T(8,128)} %drive_hbm.1, f32[64,512]{1,0:T(8,128)} %loads_hbm.1, bf16[32,256,256]{2,1,0:T(8,128)(2,1)} %tiles_hbm.1, bf16[1024,512]{1,0:T(8,128)(2,1)} %skin_hbm.1, ...), custom_call_target="tpu_custom_call" | custom-call | tf_op jit(solution)/shard_map/pallas_call | solution.py:544
  41.2 1.6 %copy.14 = f32[64,512]{1,0:T(8,128)} copy(f32[64,512]{1,0:T(8,128)} %get-tuple-element.4) | data formatting | bytes 262144
  42.8 1.6 %copy.15 = f32[64,512]{1,0:T(8,128)} copy(f32[64,512]{1,0:T(8,128)} %get-tuple-element.5) | data formatting | bytes 262144

commit v3 on v2

--- a/solution.py
+++ b/solution.py
@@ -137,6 +137,8 @@
     skin_hbm,
     skout_hbm,
     trans_hbm,
+    response_hbm,
+    sensitivity_hbm,
     response_ref,
     sensitivity_ref,
     tile_row_ref,
@@ -287,6 +289,17 @@
     grad_both = jnp.concatenate([grad_high, grad_rest], axis=0)
     excite = gradient.shape[0]
 
+    def adjoint_term(target, j):
+        index = lax.rem(b - target + clusters, clusters) - 1
+        both = dot_nn(grad_both, trans_low[index, :, j * share : (j + 1) * share])
+        return both[:excite] + both[excite:]
+
+    sib_copies = []
+    for o in range(chips):
+        for j in range(rows):
+            sib_send[o, j] = adjoint_term(blk_at(o, 1 - core), j).astype(bf16)
+        sib_copies.append(send(sib_send.at[o], sib_recv.at[o], sib_sem.at[o], sibling, r))
+
     for copy in charge_copies:
         copy.wait_recv()
     charge = charge_part[r]
@@ -312,19 +325,6 @@
         for o in range(1, rows)
     ]
 
-    def adjoint_term(target, j):
-        index = lax.rem(b - target + clusters, clusters) - 1
-        both = dot_nn(grad_both, trans_low[index, :, j * share : (j + 1) * share])
-        return both[:excite] + both[excite:]
-
-    sib_copies = []
-    for o in range(chips):
-        for j in range(rows):
-            sib_send[o, j] = adjoint_term(blk_at(o, 1 - core), j).astype(bf16)
-        sib_copies.append(send(sib_send.at[o], sib_recv.at[o], sib_sem.at[o], sibling, r))
-    for z in range(1, rows):
-        qz_copies[z - 1].wait_recv()
-        plane_q[z], sibling_q[z] = send_quarter_to_plane(z)
     plane_copies = []
     for o in range(1, chips):
         terms = [adjoint_term(blk_at(o, core), j) for j in range(rows)]
@@ -341,6 +341,10 @@
             )
         )
 
+    for z in range(1, rows):
+        qz_copies[z - 1].wait_recv()
+        plane_q[z], sibling_q[z] = send_quarter_to_plane(z)
+
     near_adj[...] = jnp.zeros_like(near_adj)
     near_fwd[...] = jnp.zeros_like(near_fwd)
     get_tiles.wait()
@@ -379,6 +383,20 @@
 
     groups = cap // GROUP
     lax.fori_loop(0, groups, adjoint_group, 0)
+    sib_copies[0].wait_recv()
+    for copy in plane_copies:
+        copy.wait_recv()
+    for j in range(rows):
+        total = sib_recv[0, j].astype(f32)
+        for o in range(chips - 1):
+            total += plane_recv[o, j].astype(f32)
+        adj_part[j] = total
+        adj_send[j] = total.astype(bf16)
+    adj_copies = [
+        send(adj_send.at[row_at(o)], adj_recv.at[o - 1], adj_sem.at[o - 1], b, row_at(o))
+        for o in range(1, rows)
+    ]
+
     for c in range(column_blocks):
         near_send[c] = near_adj[c].astype(bf16)
     near_copies = [
@@ -400,7 +418,16 @@
 
     for copy in drive_copies:
         copy.wait_recv()
-    lax.fori_loop(0, groups // 4, forward_group, 0)
+    lax.fori_loop(0, groups // 2, forward_group, 0)
+
+    for copy in adj_copies:
+        copy.wait_recv()
+    adjoint = adj_part[r]
+    for o in range(rows - 1):
+        adjoint += adj_recv[o].astype(f32)
+    adj_all[r] = adjoint.astype(bf16)
+    piece = adj_all.at[r]
+    adjall_copies = [send(piece, piece, adjall_sem.at[o - 1], b, row_at(o)) for o in range(1, rows)]
 
     for z in range(rows):
         for copy in sibling_q[z]:
@@ -414,32 +441,7 @@
     piece = pot_all.at[r]
     pot_copies = [send(piece, piece, pot_sem.at[o - 1], b, row_at(o)) for o in range(1, rows)]
 
-    sib_copies[0].wait_recv()
-    for copy in plane_copies:
-        copy.wait_recv()
-    for j in range(rows):
-        total = sib_recv[0, j].astype(f32)
-        for o in range(chips - 1):
-            total += plane_recv[o, j].astype(f32)
-        adj_part[j] = total
-        adj_send[j] = total.astype(bf16)
-    adj_copies = [
-        send(adj_send.at[row_at(o)], adj_recv.at[o - 1], adj_sem.at[o - 1], b, row_at(o))
-        for o in range(1, rows)
-    ]
-
-    lax.fori_loop(groups // 4, groups // 4 * 3, forward_group, 0)
-
-    for copy in adj_copies:
-        copy.wait_recv()
-    adjoint = adj_part[r]
-    for o in range(rows - 1):
-        adjoint += adj_recv[o].astype(f32)
-    adj_all[r] = adjoint.astype(bf16)
-    piece = adj_all.at[r]
-    adjall_copies = [send(piece, piece, adjall_sem.at[o - 1], b, row_at(o)) for o in range(1, rows)]
-
-    lax.fori_loop(groups // 4 * 3, groups, forward_group, 0)
+    lax.fori_loop(groups // 2, groups, forward_group, 0)
 
     for copy in near_copies:
         copy.wait_recv()
@@ -457,6 +459,7 @@
             block = skout[j * share : (j + 1) * share, i * size : (i + 1) * size]
             total += dot_nn(pot_all[j], block)
         response_ref[:, i * size : (i + 1) * size] = total
+    put_response = fetch(response_ref, response_hbm)
     for copy in adjall_copies:
         copy.wait_recv()
     for i in range(row_blocks):
@@ -465,8 +468,22 @@
             block = skin[j * share : (j + 1) * share, i * size : (i + 1) * size]
             total += dot_nn(adj_all[j], block)
         sensitivity_ref[:, i * size : (i + 1) * size] = total
+    put_sensitivity = fetch(sensitivity_ref, sensitivity_hbm)
     for copy in sent:
         copy.wait_send()
+    put_response.wait()
+    put_sensitivity.wait()
+
+
+def landing(response, sensitivity, response_out, sensitivity_out, sem):
+    copies = [
+        pltpu.make_async_copy(response, response_out, sem.at[0]),
+        pltpu.make_async_copy(sensitivity, sensitivity_out, sem.at[1]),
+    ]
+    for copy in copies:
+        copy.start()
+    for copy in copies:
+        copy.wait()
 
 
 def fused_plan(
@@ -493,6 +510,8 @@
     sends = 7 * others + rows * (chips - 1) + rows * chips + chips + chips - 1 + others
     vmem, dma = pltpu.VMEM, pltpu.SemaphoreType.DMA
     scratch = [
+        vmem((excite, panels), f32),
+        vmem((excite, panels), f32),
         pltpu.SMEM(tile_rows.shape, jnp.int32),
         pltpu.SMEM(tile_cols.shape, jnp.int32),
         vmem((excite, panels), f32),
@@ -524,7 +543,7 @@
         vmem((blocks, excite, size), f32),
         vmem((blocks, excite, size), bf16),
         vmem((others, row_blocks, excite, size), bf16),
-        dma((offsets + 7,)),
+        dma((offsets + 9,)),
         dma((sends,)),
         dma((others,)),
         dma((others,)),
@@ -539,13 +558,12 @@
         dma((others,)),
         dma((others,)),
     ]
-    whole_vmem = pl.BlockSpec(memory_space=pltpu.VMEM)
     anywhere = pl.BlockSpec(memory_space=pl.ANY)
-    return pl.pallas_call(
+    results = pl.pallas_call(
         functools.partial(kernel, rows, clusters),
         out_shape=[jax.ShapeDtypeStruct((excite, panels), f32)] * 2,
         in_specs=[pl.BlockSpec(memory_space=pltpu.SMEM)] + [anywhere] * 8,
-        out_specs=[whole_vmem] * 2,
+        out_specs=[anywhere] * 2,
         scratch_shapes=scratch,
         compiler_params=pltpu.CompilerParams(
             collective_id=0, has_side_effects=True, vmem_limit_bytes=VMEM_BYTES
@@ -561,6 +579,14 @@
         skeleton_out,
         kernels,
     )
+    return pl.pallas_call(
+        landing,
+        out_shape=[jax.ShapeDtypeStruct((excite, panels), f32)] * 2,
+        in_specs=[anywhere] * 2,
+        out_specs=[anywhere] * 2,
+        scratch_shapes=[dma((2,))],
+        compiler_params=pltpu.CompilerParams(vmem_limit_bytes=VMEM_BYTES),
+    )(*results)
 
 
 def solution(mesh):

time: 44.5 us -> 48.9 us (1.099)
  Pallas kernels: 39.9 us -> 47.4 us
  local copies, waits for them, and re-layouts: 3.14 us -> 0 us
    pallas_call x0 -> x1, Pallas kernels: none -> 9.06 us  [fused_plan(): pl.pallas_call(landing, out_shape=[jax.ShapeDtypeStruct((excite, panels),...]
    unnamed x2 -> x0, local copies, waits for them, and re-layouts: 3.14 us -> none
    pallas_call x1, Pallas kernels: 39.9 us -> 38.4 us  [fused_plan(): pl.pallas_call(functools.partial(kernel, rows, clusters), out_shape=[jax....]
where the time goes in v3:
time: 48.9 us; the launch traced here: 48.7 us
  Pallas kernels  47.4 us (97%)
  between operations  1.29 us (3%)
    pallas_call x1, Pallas kernels, fused_plan(): pl.pallas_call(functools.partial(kernel, rows, clusters), out_shape=[jax....  38.4 us
    pallas_call x1, Pallas kernels, fused_plan(): pl.pallas_call(landing, out_shape=[jax.ShapeDtypeStruct((excite, panels),...  9.06 us

profile of v3, /device:TPU:0, one launch (start us, length us, event | category | flops | bytes accessed | tf_op | source)
XLA Modules:
  0.0 48.7 jit_solution(17891757069539886213)
XLA Ops:
  1.3 38.4 %shard_map.104 = (f32[64,512]{1,0:T(8,128)}, f32[64,512]{1,0:T(8,128)}) custom-call(s32[1]{0:T(128)S(6)} %copy.11.count_ref, s32[32]{0:T(128)} %tile_row_hbm.1, s32[32]{0:T(128)} %tile_col_hbm.1, f32[64,512]{1,0:T(8,128)} %drive_hbm.1, f32[64,512]{1,0:T(8,128)} %loads_hbm.1, bf16[32,256,256]{2,1,0:T(8,128)(2,1)} %tiles_hbm.1, bf16[1024,512]{1,0:T(8,128)(2,1)} %skin_hbm.1, ...), custom_call_target="tpu_custom_call" | custom-call | tf_op jit(solution)/shard_map/pallas_call | solution.py:562
  39.6 9.1 %shard_map.105 = (f32[64,512]{1,0:T(8,128)}, f32[64,512]{1,0:T(8,128)}) custom-call(f32[64,512]{1,0:T(8,128)} %get-tuple-element.4.response, f32[64,512]{1,0:T(8,128)} %get-tuple-element.5.sensitivity), custom_call_target="tpu_custom_call" | custom-call | tf_op jit(solution)/shard_map/pallas_call | solution.py:582

commit v4 on v3

--- a/solution.py
+++ b/solution.py
@@ -171,7 +171,11 @@
     near_fwd,
     near_adj,
     near_send,
-    near_recv,
+    near_first,
+    near_pair,
+    near_mid,
+    near_back,
+    near_last,
     local_sem,
     send_sem,
     grad_sem,
@@ -227,7 +231,7 @@
 
     sent = []
 
-    def send(src, dst, recv, blk, row):
+    def send(src, dst, recv, blk, row, only=None):
         copy = pltpu.make_async_remote_copy(
             src_ref=src,
             dst_ref=dst,
@@ -236,9 +240,34 @@
             device_id=(blk, row),
             device_id_type=MESH,
         )
-        copy.start()
-        sent.append(copy)
+        if only is None:
+            copy.start()
+        else:
+            pl.when(only)(copy.start)
+        sent.append((copy, only))
         return copy
+
+    def send_later(src, dst, recv, blk, row):
+        copy = pltpu.make_async_remote_copy(
+            src_ref=src,
+            dst_ref=dst,
+            send_sem=send_sem.at[len(sent)],
+            recv_sem=recv,
+            device_id=(blk, row),
+            device_id_type=MESH,
+        )
+        sent.append((copy, inner))
+        return copy
+
+    inner = lax.rem(r + 1, rows) >= 2
+    outer = lax.rem(r + 1, rows) < 2
+    mate = r + 1 - 2 * lax.rem(r, 2)
+    opposite = rows - 1 - r
+    pair = r - lax.rem(r, 2)
+    far_pair = rows - 2 - pair
+
+    def blocks_of(row, count):
+        return pl.ds(row * row_blocks, count * row_blocks)
 
     barrier = pltpu.get_barrier_semaphore()
     partners = [(b, row_at(o)) for o in range(1, rows)]
@@ -319,11 +348,8 @@
     plane_q, sibling_q = [None] * rows, [None] * rows
     plane_q[0], sibling_q[0] = send_quarter_to_plane(0)
 
-    mine = pl.ds(r * row_blocks, row_blocks)
-    drive_copies = [
-        send(drive_all.at[mine], drive_all.at[mine], drive_sem.at[o - 1], b, row_at(o))
-        for o in range(1, rows)
-    ]
+    piece = drive_all.at[blocks_of(r, 1)]
+    drive_first = send(piece, piece, drive_sem.at[0], b, mate)
 
     plane_copies = []
     for o in range(1, chips):
@@ -345,6 +371,10 @@
         qz_copies[z - 1].wait_recv()
         plane_q[z], sibling_q[z] = send_quarter_to_plane(z)
 
+    drive_first.wait_recv()
+    piece = drive_all.at[blocks_of(pair, 2)]
+    send(piece, piece, drive_sem.at[1], b, opposite, inner)
+
     near_adj[...] = jnp.zeros_like(near_adj)
     near_fwd[...] = jnp.zeros_like(near_fwd)
     get_tiles.wait()
@@ -383,6 +413,15 @@
 
     groups = cap // GROUP
     lax.fori_loop(0, groups, adjoint_group, 0)
+    for c in range(column_blocks):
+        near_send[c] = near_adj[c].astype(bf16)
+    near_far = send(near_send.at[blocks_of(far_pair, 2)], near_pair, near_sem.at[1], b, mate, outer)
+    near_mate = send(near_send.at[blocks_of(mate, 1)], near_first, near_sem.at[0], b, mate)
+    piece = drive_all.at[blocks_of(far_pair, 2)]
+    drive_last = send_later(piece, piece, drive_sem.at[1], b, mate)
+    drive_last.wait_recv()
+    pl.when(inner)(drive_last.start)
+
     sib_copies[0].wait_recv()
     for copy in plane_copies:
         copy.wait_recv()
@@ -397,18 +436,6 @@
         for o in range(1, rows)
     ]
 
-    for c in range(column_blocks):
-        near_send[c] = near_adj[c].astype(bf16)
-    near_copies = [
-        send(
-            near_send.at[pl.ds(row_at(o) * row_blocks, row_blocks)],
-            near_recv.at[o - 1],
-            near_sem.at[o - 1],
-            b,
-            row_at(o),
-        )
-        for o in range(1, rows)
-    ]
 
     for z in range(rows):
         for o in range(1, chips):
@@ -416,8 +443,14 @@
             piece = q_all.at[row_at(-z), blk_at(-o, core)]
             sibling_q[z].append(send(piece, piece, qs_sem.at[z, o], sibling, r))
 
-    for copy in drive_copies:
-        copy.wait_recv()
+    @pl.when(inner)
+    def _():
+        near_far.wait_recv()
+        for i in range(2 * row_blocks):
+            total = near_adj[far_pair * row_blocks + i] + near_pair[i].astype(f32)
+            near_mid[i] = total.astype(bf16)
+
+    near_cross = send(near_mid, near_back, near_sem.at[2], b, opposite, inner)
     lax.fori_loop(0, groups // 2, forward_group, 0)
 
     for copy in adj_copies:
@@ -428,6 +461,10 @@
     adj_all[r] = adjoint.astype(bf16)
     piece = adj_all.at[r]
     adjall_copies = [send(piece, piece, adjall_sem.at[o - 1], b, row_at(o)) for o in range(1, rows)]
+
+    pl.when(inner)(near_cross.wait_recv)
+    part = near_back.at[pl.ds((mate - pair) * row_blocks, row_blocks)]
+    near_give = send(part, near_last, near_sem.at[3], b, mate, inner)
 
     for z in range(rows):
         for copy in sibling_q[z]:
@@ -443,13 +480,17 @@
 
     lax.fori_loop(groups // 2, groups, forward_group, 0)
 
-    for copy in near_copies:
-        copy.wait_recv()
+    near_mate.wait_recv()
+    pl.when(outer)(near_give.wait_recv)
+
+    @pl.when(inner)
+    def _():
+        for i in range(row_blocks):
+            near_last[i] = near_back[(r - pair) * row_blocks + i]
+
     for i in range(row_blocks):
-        total = near_adj[r * row_blocks + i]
-        for o in range(rows - 1):
-            total += near_recv[o, i].astype(f32)
-        near_adj[r * row_blocks + i] = total
+        total = near_adj[r * row_blocks + i] + near_first[i].astype(f32)
+        near_adj[r * row_blocks + i] = total + near_last[i].astype(f32)
 
     for copy in pot_copies:
         copy.wait_recv()
@@ -469,21 +510,18 @@
             total += dot_nn(adj_all[j], block)
         sensitivity_ref[:, i * size : (i + 1) * size] = total
     put_sensitivity = fetch(sensitivity_ref, sensitivity_hbm)
-    for copy in sent:
-        copy.wait_send()
+    for copy, only in sent:
+        if only is None:
+            copy.wait_send()
+        else:
+            pl.when(only)(copy.wait_send)
     put_response.wait()
     put_sensitivity.wait()
 
 
-def landing(response, sensitivity, response_out, sensitivity_out, sem):
-    copies = [
-        pltpu.make_async_copy(response, response_out, sem.at[0]),
-        pltpu.make_async_copy(sensitivity, sensitivity_out, sem.at[1]),
-    ]
-    for copy in copies:
-        copy.start()
-    for copy in copies:
-        copy.wait()
+def landing(response, sensitivity, response_out, sensitivity_out):
+    response_out[...] = response[...]
+    sensitivity_out[...] = sensitivity[...]
 
 
 def fused_plan(
@@ -507,7 +545,7 @@
     row_blocks = panels // size
     blocks = rows * row_blocks
     others = rows - 1
-    sends = 7 * others + rows * (chips - 1) + rows * chips + chips + chips - 1 + others
+    sends = 6 * others + 3 + 4 + rows * (chips - 1) + rows * chips + chips + chips - 1
     vmem, dma = pltpu.VMEM, pltpu.SemaphoreType.DMA
     scratch = [
         vmem((excite, panels), f32),
@@ -542,12 +580,16 @@
         vmem((row_blocks, excite, size), f32),
         vmem((blocks, excite, size), f32),
         vmem((blocks, excite, size), bf16),
-        vmem((others, row_blocks, excite, size), bf16),
+        vmem((row_blocks, excite, size), bf16),
+        vmem((2 * row_blocks, excite, size), bf16),
+        vmem((2 * row_blocks, excite, size), bf16),
+        vmem((2 * row_blocks, excite, size), bf16),
+        vmem((row_blocks, excite, size), bf16),
         dma((offsets + 9,)),
         dma((sends,)),
         dma((others,)),
         dma((others,)),
-        dma((others,)),
+        dma((2,)),
         dma((others,)),
         dma((rows, chips - 1)),
         dma((rows, chips)),
@@ -556,8 +598,9 @@
         dma((others,)),
         dma((others,)),
         dma((others,)),
-        dma((others,)),
+        dma((4,)),
     ]
+    whole_vmem = pl.BlockSpec(memory_space=pltpu.VMEM)
     anywhere = pl.BlockSpec(memory_space=pl.ANY)
     results = pl.pallas_call(
         functools.partial(kernel, rows, clusters),
@@ -582,9 +625,8 @@
     return pl.pallas_call(
         landing,
         out_shape=[jax.ShapeDtypeStruct((excite, panels), f32)] * 2,
-        in_specs=[anywhere] * 2,
-        out_specs=[anywhere] * 2,
-        scratch_shapes=[dma((2,))],
+        in_specs=[whole_vmem] * 2,
+        out_specs=[whole_vmem] * 2,
         compiler_params=pltpu.CompilerParams(vmem_limit_bytes=VMEM_BYTES),
     )(*results)
 

time: 48.9 us -> 43.7 us (0.89)
  Pallas kernels: 47.4 us -> 42.3 us
    pallas_call x1, Pallas kernels: 9.06 us -> 1.68 us  [fused_plan(): pl.pallas_call(landing, out_shape=[jax.ShapeDtypeStruct((excite, panels),...]
    pallas_call x1, Pallas kernels: 38.4 us -> 40.6 us  [fused_plan(): pl.pallas_call(functools.partial(kernel, rows, clusters), out_shape=[jax....]
where the time goes in v4:
time: 43.7 us; the launch traced here: 43.6 us
  Pallas kernels  42.3 us (97%)
  between operations  1.29 us (3%)
    pallas_call x1, Pallas kernels, fused_plan(): pl.pallas_call(functools.partial(kernel, rows, clusters), out_shape=[jax....  40.6 us
    pallas_call x1, Pallas kernels, fused_plan(): pl.pallas_call(landing, out_shape=[jax.ShapeDtypeStruct((excite, panels),...  1.68 us

profile of v4, /device:TPU:0, one launch (start us, length us, event | category | flops | bytes accessed | tf_op | source)
XLA Modules:
  0.0 43.6 jit_solution(14697201088927556682)
XLA Ops:
  1.3 40.6 %shard_map.104 = (f32[64,512]{1,0:T(8,128)}, f32[64,512]{1,0:T(8,128)}) custom-call(s32[1]{0:T(128)S(6)} %copy.11.count_ref, s32[32]{0:T(128)} %tile_row_hbm.1, s32[32]{0:T(128)} %tile_col_hbm.1, f32[64,512]{1,0:T(8,128)} %drive_hbm.1, f32[64,512]{1,0:T(8,128)} %loads_hbm.1, bf16[32,256,256]{2,1,0:T(8,128)(2,1)} %tiles_hbm.1, bf16[1024,512]{1,0:T(8,128)(2,1)} %skin_hbm.1, ...), custom_call_target="tpu_custom_call" | custom-call | tf_op jit(solution)/shard_map/pallas_call | solution.py:605
  41.9 1.7 %shard_map.105 = (f32[64,512]{1,0:T(8,128)}, f32[64,512]{1,0:T(8,128)}) custom-call(f32[64,512]{1,0:T(8,128)} %get-tuple-element.4.response, f32[64,512]{1,0:T(8,128)} %get-tuple-element.5.sensitivity), custom_call_target="tpu_custom_call" | custom-call | tf_op jit(solution)/shard_map/pallas_call | solution.py:625

commit v5 on v3

--- a/solution.py
+++ b/solution.py
@@ -305,19 +305,10 @@
     charge = charge_part[r]
     for o in range(rows - 1):
         charge += charge_recv[o].astype(f32)
-    q_all[r, b] = charge.astype(bf16)
-
-    def send_quarter_to_plane(z):
-        piece = q_all.at[row_at(-z), b]
-        copies = [
-            send(piece, piece, qp_sem.at[z, o - 1], blk_at(o, core), r) for o in range(1, chips)
-        ]
-        return copies, [send(piece, piece, qs_sem.at[z, 0], sibling, r)]
-
-    piece = q_all.at[r, b]
+    q_all[b, r] = charge.astype(bf16)
+
+    piece = q_all.at[b, r]
     qz_copies = [send(piece, piece, qz_sem.at[o - 1], b, row_at(o)) for o in range(1, rows)]
-    plane_q, sibling_q = [None] * rows, [None] * rows
-    plane_q[0], sibling_q[0] = send_quarter_to_plane(0)
 
     mine = pl.ds(r * row_blocks, row_blocks)
     drive_copies = [
@@ -341,9 +332,11 @@
             )
         )
 
-    for z in range(1, rows):
-        qz_copies[z - 1].wait_recv()
-        plane_q[z], sibling_q[z] = send_quarter_to_plane(z)
+    for copy in qz_copies:
+        copy.wait_recv()
+    piece = q_all.at[b]
+    plane_q = [send(piece, piece, qp_sem.at[o - 1], blk_at(o, core), r) for o in range(1, chips)]
+    sibling_q = [send(piece, piece, qs_sem.at[0], sibling, r)]
 
     near_adj[...] = jnp.zeros_like(near_adj)
     near_fwd[...] = jnp.zeros_like(near_fwd)
@@ -410,11 +403,10 @@
         for o in range(1, rows)
     ]
 
-    for z in range(rows):
-        for o in range(1, chips):
-            plane_q[z][o - 1].wait_recv()
-            piece = q_all.at[row_at(-z), blk_at(-o, core)]
-            sibling_q[z].append(send(piece, piece, qs_sem.at[z, o], sibling, r))
+    for o in range(1, chips):
+        plane_q[o - 1].wait_recv()
+        piece = q_all.at[blk_at(-o, core)]
+        sibling_q.append(send(piece, piece, qs_sem.at[o], sibling, r))
 
     for copy in drive_copies:
         copy.wait_recv()
@@ -429,13 +421,12 @@
     piece = adj_all.at[r]
     adjall_copies = [send(piece, piece, adjall_sem.at[o - 1], b, row_at(o)) for o in range(1, rows)]
 
-    for z in range(rows):
-        for copy in sibling_q[z]:
-            copy.wait_recv()
+    for copy in sibling_q:
+        copy.wait_recv()
     potential = jnp.zeros((excite, share), f32)
     for j in range(rows):
         for d in range(1, offsets + 1):
-            source = q_all[j, lax.rem(b - d + clusters, clusters)]
+            source = q_all[lax.rem(b - d + clusters, clusters), j]
             potential += dot_nt(source, trans_low[d - 1, :, j * share : (j + 1) * share])
     pot_all[r] = potential.astype(bf16)
     piece = pot_all.at[r]
@@ -475,15 +466,9 @@
     put_sensitivity.wait()
 
 
-def landing(response, sensitivity, response_out, sensitivity_out, sem):
-    copies = [
-        pltpu.make_async_copy(response, response_out, sem.at[0]),
-        pltpu.make_async_copy(sensitivity, sensitivity_out, sem.at[1]),
-    ]
-    for copy in copies:
-        copy.start()
-    for copy in copies:
-        copy.wait()
+def landing(response, sensitivity, response_out, sensitivity_out):
+    response_out[...] = response[...]
+    sensitivity_out[...] = sensitivity[...]
 
 
 def fused_plan(
@@ -507,7 +492,7 @@
     row_blocks = panels // size
     blocks = rows * row_blocks
     others = rows - 1
-    sends = 7 * others + rows * (chips - 1) + rows * chips + chips + chips - 1 + others
+    sends = 7 * others + 3 * chips - 1 + chips - 1 + others
     vmem, dma = pltpu.VMEM, pltpu.SemaphoreType.DMA
     scratch = [
         vmem((excite, panels), f32),
@@ -529,7 +514,7 @@
         vmem((rows, excite, share), f32),
         vmem((rows, excite, share), bf16),
         vmem((others, excite, share), bf16),
-        vmem((rows, clusters, excite, share), bf16),
+        vmem((clusters, rows, excite, share), bf16),
         vmem((chips, rows, excite, share), bf16),
         vmem((chips, rows, excite, share), bf16),
         vmem((chips - 1, rows, excite, share), bf16),
@@ -549,8 +534,8 @@
         dma((others,)),
         dma((others,)),
         dma((others,)),
-        dma((rows, chips - 1)),
-        dma((rows, chips)),
+        dma((chips - 1,)),
+        dma((chips,)),
         dma((chips,)),
         dma((chips - 1,)),
         dma((others,)),
@@ -558,6 +543,7 @@
         dma((others,)),
         dma((others,)),
     ]
+    whole_vmem = pl.BlockSpec(memory_space=pltpu.VMEM)
     anywhere = pl.BlockSpec(memory_space=pl.ANY)
     results = pl.pallas_call(
         functools.partial(kernel, rows, clusters),
@@ -582,9 +568,8 @@
     return pl.pallas_call(
         landing,
         out_shape=[jax.ShapeDtypeStruct((excite, panels), f32)] * 2,
-        in_specs=[anywhere] * 2,
-        out_specs=[anywhere] * 2,
-        scratch_shapes=[dma((2,))],
+        in_specs=[whole_vmem] * 2,
+        out_specs=[whole_vmem] * 2,
         compiler_params=pltpu.CompilerParams(vmem_limit_bytes=VMEM_BYTES),
     )(*results)
 

time: 48.9 us -> 40.4 us (0.83)
  Pallas kernels: 47.4 us -> 38.9 us
    pallas_call x1, Pallas kernels: 9.06 us -> 1.68 us  [fused_plan(): pl.pallas_call(landing, out_shape=[jax.ShapeDtypeStruct((excite, panels),...]
    pallas_call x1, Pallas kernels: 38.4 us -> 37.3 us  [fused_plan(): pl.pallas_call(functools.partial(kernel, rows, clusters), out_shape=[jax....]
where the time goes in v5:
time: 40.4 us; the launch traced here: 40.2 us
  Pallas kernels  38.9 us (96%)
  between operations  1.29 us (3%)
    pallas_call x1, Pallas kernels, fused_plan(): pl.pallas_call(functools.partial(kernel, rows, clusters), out_shape=[jax....  37.3 us
    pallas_call x1, Pallas kernels, fused_plan(): pl.pallas_call(landing, out_shape=[jax.ShapeDtypeStruct((excite, panels),...  1.68 us

profile of v5, /device:TPU:0, one launch (start us, length us, event | category | flops | bytes accessed | tf_op | source)
XLA Modules:
  0.0 40.2 jit_solution(8434827891235401579)
XLA Ops:
  1.3 37.3 %shard_map.104 = (f32[64,512]{1,0:T(8,128)}, f32[64,512]{1,0:T(8,128)}) custom-call(s32[1]{0:T(128)S(6)} %copy.11.count_ref, s32[32]{0:T(128)} %tile_row_hbm.1, s32[32]{0:T(128)} %tile_col_hbm.1, f32[64,512]{1,0:T(8,128)} %drive_hbm.1, f32[64,512]{1,0:T(8,128)} %loads_hbm.1, bf16[32,256,256]{2,1,0:T(8,128)(2,1)} %tiles_hbm.1, bf16[1024,512]{1,0:T(8,128)(2,1)} %skin_hbm.1, ...), custom_call_target="tpu_custom_call" | custom-call | tf_op jit(solution)/shard_map/pallas_call | solution.py:548
  38.5 1.7 %shard_map.105 = (f32[64,512]{1,0:T(8,128)}, f32[64,512]{1,0:T(8,128)}) custom-call(f32[64,512]{1,0:T(8,128)} %get-tuple-element.4.response, f32[64,512]{1,0:T(8,128)} %get-tuple-element.5.sensitivity), custom_call_target="tpu_custom_call" | custom-call | tf_op jit(solution)/shard_map/pallas_call | solution.py:568

commit v6 on v5

--- a/solution.py
+++ b/solution.py
@@ -294,21 +294,23 @@
         both = dot_nn(grad_both, trans_low[index, :, j * share : (j + 1) * share])
         return both[:excite] + both[excite:]
 
-    sib_copies = []
-    for o in range(chips):
+    sib_copies = [None] * chips
+    for o in [*range(1, chips), 0]:
         for j in range(rows):
             sib_send[o, j] = adjoint_term(blk_at(o, 1 - core), j).astype(bf16)
-        sib_copies.append(send(sib_send.at[o], sib_recv.at[o], sib_sem.at[o], sibling, r))
+        sib_copies[o] = send(sib_send.at[o], sib_recv.at[o], sib_sem.at[o], sibling, r)
 
     for copy in charge_copies:
         copy.wait_recv()
     charge = charge_part[r]
     for o in range(rows - 1):
         charge += charge_recv[o].astype(f32)
-    q_all[b, r] = charge.astype(bf16)
-
-    piece = q_all.at[b, r]
-    qz_copies = [send(piece, piece, qz_sem.at[o - 1], b, row_at(o)) for o in range(1, rows)]
+    q_all[b, 0] = charge.astype(bf16)
+    piece = q_all.at[b, 0]
+    qz_copies = [
+        send(piece, q_all.at[b, o], qz_sem.at[o - 1], b, row_at(o)) for o in range(1, rows)
+    ]
+    plane_q = [send(piece, piece, qp_sem.at[0, o - 1], blk_at(o, core), r) for o in range(1, chips)]
 
     mine = pl.ds(r * row_blocks, row_blocks)
     drive_copies = [
@@ -332,12 +334,6 @@
             )
         )
 
-    for copy in qz_copies:
-        copy.wait_recv()
-    piece = q_all.at[b]
-    plane_q = [send(piece, piece, qp_sem.at[o - 1], blk_at(o, core), r) for o in range(1, chips)]
-    sibling_q = [send(piece, piece, qs_sem.at[0], sibling, r)]
-
     near_adj[...] = jnp.zeros_like(near_adj)
     near_fwd[...] = jnp.zeros_like(near_fwd)
     get_tiles.wait()
@@ -375,7 +371,16 @@
         return carry
 
     groups = cap // GROUP
-    lax.fori_loop(0, groups, adjoint_group, 0)
+    lax.fori_loop(0, groups // 2, adjoint_group, 0)
+
+    for copy in qz_copies:
+        copy.wait_recv()
+    piece = q_all.at[b, pl.ds(1, rows - 1)]
+    plane_q += [send(piece, piece, qp_sem.at[1, o - 1], blk_at(o, core), r) for o in range(1, chips)]
+    piece = q_all.at[b]
+    sibling_q = [send(piece, piece, qs_sem.at[0], sibling, r)]
+
+    lax.fori_loop(groups // 2, groups, adjoint_group, 0)
     sib_copies[0].wait_recv()
     for copy in plane_copies:
         copy.wait_recv()
@@ -405,6 +410,7 @@
 
     for o in range(1, chips):
         plane_q[o - 1].wait_recv()
+        plane_q[chips - 2 + o].wait_recv()
         piece = q_all.at[blk_at(-o, core)]
         sibling_q.append(send(piece, piece, qs_sem.at[o], sibling, r))
 
@@ -424,10 +430,11 @@
     for copy in sibling_q:
         copy.wait_recv()
     potential = jnp.zeros((excite, share), f32)
-    for j in range(rows):
+    for z in range(rows):
+        columns = pl.ds(pl.multiple_of(row_at(-z) * share, share), share)
         for d in range(1, offsets + 1):
-            source = q_all[lax.rem(b - d + clusters, clusters), j]
-            potential += dot_nt(source, trans_low[d - 1, :, j * share : (j + 1) * share])
+            source = q_all[lax.rem(b - d + clusters, clusters), z]
+            potential += dot_nt(source, trans_low[d - 1, :, columns])
     pot_all[r] = potential.astype(bf16)
     piece = pot_all.at[r]
     pot_copies = [send(piece, piece, pot_sem.at[o - 1], b, row_at(o)) for o in range(1, rows)]
@@ -492,7 +499,7 @@
     row_blocks = panels // size
     blocks = rows * row_blocks
     others = rows - 1
-    sends = 7 * others + 3 * chips - 1 + chips - 1 + others
+    sends = 7 * others + 4 * chips - 2 + chips - 1 + others
     vmem, dma = pltpu.VMEM, pltpu.SemaphoreType.DMA
     scratch = [
         vmem((excite, panels), f32),
@@ -534,7 +541,7 @@
         dma((others,)),
         dma((others,)),
         dma((others,)),
-        dma((chips - 1,)),
+        dma((2, chips - 1)),
         dma((chips,)),
         dma((chips,)),
         dma((chips - 1,)),

time: 40.4 us -> 40.8 us (level)
  Pallas kernels: 38.9 us -> 39.4 us
    pallas_call x1, Pallas kernels: 37.3 us -> 37.7 us  [fused_plan(): pl.pallas_call(functools.partial(kernel, rows, clusters), out_shape=[jax....]
where the time goes in v6:
time: 40.8 us; the launch traced here: 40.7 us
  Pallas kernels  39.4 us (97%)
  between operations  1.29 us (3%)
    pallas_call x1, Pallas kernels, fused_plan(): pl.pallas_call(functools.partial(kernel, rows, clusters), out_shape=[jax....  37.7 us
    pallas_call x1, Pallas kernels, fused_plan(): pl.pallas_call(landing, out_shape=[jax.ShapeDtypeStruct((excite, panels),...  1.68 us

profile of v6, /device:TPU:0, one launch (start us, length us, event | category | flops | bytes accessed | tf_op | source)
XLA Modules:
  0.0 40.7 jit_solution(4994845375698282334)
XLA Ops:
  1.3 37.7 %shard_map.104 = (f32[64,512]{1,0:T(8,128)}, f32[64,512]{1,0:T(8,128)}) custom-call(s32[1]{0:T(128)S(6)} %copy.11.count_ref, s32[32]{0:T(128)} %tile_row_hbm.1, s32[32]{0:T(128)} %tile_col_hbm.1, f32[64,512]{1,0:T(8,128)} %drive_hbm.1, f32[64,512]{1,0:T(8,128)} %loads_hbm.1, bf16[32,256,256]{2,1,0:T(8,128)(2,1)} %tiles_hbm.1, bf16[1024,512]{1,0:T(8,128)(2,1)} %skin_hbm.1, ...), custom_call_target="tpu_custom_call" | custom-call | tf_op jit(solution)/shard_map/pallas_call | solution.py:555
  39.0 1.7 %shard_map.105 = (f32[64,512]{1,0:T(8,128)}, f32[64,512]{1,0:T(8,128)}) custom-call(f32[64,512]{1,0:T(8,128)} %get-tuple-element.4.response, f32[64,512]{1,0:T(8,128)} %get-tuple-element.5.sensitivity), custom_call_target="tpu_custom_call" | custom-call | tf_op jit(solution)/shard_map/pallas_call | solution.py:575

commit v7 on v6

--- a/solution.py
+++ b/solution.py
@@ -218,13 +218,6 @@
     get_out = fetch(skout_hbm, skout)
     get_drive = fetch(drive_hbm, drive_ref)
     get_in = fetch(skin_hbm, skin)
-    get_trans = [fetch(trans_hbm.at[d], trans.at[d]) for d in range(offsets)]
-    get_tiles = fetch(tiles_hbm, tiles)
-    get_lists = [
-        fetch(tile_row_hbm, tile_row_ref),
-        fetch(tile_col_hbm, tile_col_ref),
-    ]
-
     sent = []
 
     def send(src, dst, recv, blk, row):
@@ -252,6 +245,11 @@
         loads_low[i] = loads_ref[:, i * size : (i + 1) * size].astype(bf16)
     loads_wide = loads_ref[...].astype(bf16)
     get_out.wait()
+    get_trans = [fetch(trans_hbm.at[d], trans.at[d]) for d in range(offsets)]
+    get_lists = [
+        fetch(tile_row_hbm, tile_row_ref),
+        fetch(tile_col_hbm, tile_col_ref),
+    ]
     for j in range(rows):
         part = dot_nt(loads_wide, skout[j * share : (j + 1) * share, :])
         grad_part[j] = part
@@ -266,6 +264,7 @@
         drive_all[r * row_blocks + i] = drive_ref[:, i * size : (i + 1) * size].astype(bf16)
     drive_wide = drive_ref[...].astype(bf16)
     get_in.wait()
+    get_tiles = fetch(tiles_hbm, tiles)
     for j in range(rows):
         part = dot_nt(drive_wide, skin[j * share : (j + 1) * share, :])
         charge_part[j] = part
@@ -380,7 +379,6 @@
     piece = q_all.at[b]
     sibling_q = [send(piece, piece, qs_sem.at[0], sibling, r)]
 
-    lax.fori_loop(groups // 2, groups, adjoint_group, 0)
     sib_copies[0].wait_recv()
     for copy in plane_copies:
         copy.wait_recv()
@@ -395,6 +393,13 @@
         for o in range(1, rows)
     ]
 
+    for o in range(1, chips):
+        plane_q[o - 1].wait_recv()
+        plane_q[chips - 2 + o].wait_recv()
+        piece = q_all.at[blk_at(-o, core)]
+        sibling_q.append(send(piece, piece, qs_sem.at[o], sibling, r))
+
+    lax.fori_loop(groups // 2, groups, adjoint_group, 0)
     for c in range(column_blocks):
         near_send[c] = near_adj[c].astype(bf16)
     near_copies = [
@@ -408,15 +413,9 @@
         for o in range(1, rows)
     ]
 
-    for o in range(1, chips):
-        plane_q[o - 1].wait_recv()
-        plane_q[chips - 2 + o].wait_recv()
-        piece = q_all.at[blk_at(-o, core)]
-        sibling_q.append(send(piece, piece, qs_sem.at[o], sibling, r))
-
     for copy in drive_copies:
         copy.wait_recv()
-    lax.fori_loop(0, groups // 2, forward_group, 0)
+    lax.fori_loop(0, groups // 4, forward_group, 0)
 
     for copy in adj_copies:
         copy.wait_recv()
@@ -439,7 +438,7 @@
     piece = pot_all.at[r]
     pot_copies = [send(piece, piece, pot_sem.at[o - 1], b, row_at(o)) for o in range(1, rows)]
 
-    lax.fori_loop(groups // 2, groups, forward_group, 0)
+    lax.fori_loop(groups // 4, groups, forward_group, 0)
 
     for copy in near_copies:
         copy.wait_recv()

time: 40.8 us -> 43.2 us (1.059)
  Pallas kernels: 39.4 us -> 41.7 us
    pallas_call x1, Pallas kernels: 37.7 us -> 40.1 us  [fused_plan(): pl.pallas_call(functools.partial(kernel, rows, clusters), out_shape=[jax....]
where the time goes in v7:
time: 43.2 us; the launch traced here: 43 us
  Pallas kernels  41.7 us (97%)
  between operations  1.29 us (3%)
    pallas_call x1, Pallas kernels, fused_plan(): pl.pallas_call(functools.partial(kernel, rows, clusters), out_shape=[jax....  40.1 us
    pallas_call x1, Pallas kernels, fused_plan(): pl.pallas_call(landing, out_shape=[jax.ShapeDtypeStruct((excite, panels),...  1.68 us

profile of v7, /device:TPU:0, one launch (start us, length us, event | category | flops | bytes accessed | tf_op | source)
XLA Modules:
  0.0 43.0 jit_solution(8907077172655502278)
XLA Ops:
  1.3 40.1 %shard_map.104 = (f32[64,512]{1,0:T(8,128)}, f32[64,512]{1,0:T(8,128)}) custom-call(s32[1]{0:T(128)S(6)} %copy.11.count_ref, s32[32]{0:T(128)} %tile_row_hbm.1, s32[32]{0:T(128)} %tile_col_hbm.1, f32[64,512]{1,0:T(8,128)} %drive_hbm.1, f32[64,512]{1,0:T(8,128)} %loads_hbm.1, bf16[32,256,256]{2,1,0:T(8,128)(2,1)} %tiles_hbm.1, bf16[1024,512]{1,0:T(8,128)(2,1)} %skin_hbm.1, ...), custom_call_target="tpu_custom_call" | custom-call | tf_op jit(solution)/shard_map/pallas_call | solution.py:554
  41.3 1.7 %shard_map.105 = (f32[64,512]{1,0:T(8,128)}, f32[64,512]{1,0:T(8,128)}) custom-call(f32[64,512]{1,0:T(8,128)} %get-tuple-element.4.response, f32[64,512]{1,0:T(8,128)} %get-tuple-element.5.sensitivity), custom_call_target="tpu_custom_call" | custom-call | tf_op jit(solution)/shard_map/pallas_call | solution.py:574
